TPU v7x, 256 devices: a whole 4x4x8 slice. The times are simulated.
256 devices in a mesh: pipe: 4 (over y_lo, core), expert: 64 (over z, y_hi, x).
Axes of the slice: x: 4, y: 4 (y_hi: 2, y_lo: 2; y = y_hi * 2 + y_lo), z: 8, core: 2. Of those that a mesh axis runs over, the one named last changes fastest.
Arguments:
- east_prev: bfloat16 [4, 4096, 7168], P('pipe', 'expert'), may hold values from -6 to 6
- west_prev: bfloat16 [4, 4096, 7168], P('pipe', 'expert'), may hold values from -6 to 6
- east_routes: int32 [4, 4096, 8], P('pipe', 'expert'), may hold values from 0 to 255, all different within a row; in each aligned block of 64 rows (0 to 63, 64 to 127, ..., all dimensions but the last counted through in order) at most 4 rows name the same one
- west_routes: int32 [4, 4096, 8], P('pipe', 'expert'), may hold values from 0 to 255, all different within a row; in each aligned block of 64 rows (0 to 63, 64 to 127, ..., all dimensions but the last counted through in order) at most 4 rows name the same one
- east_affinity: float32 [4, 4096, 8], P('pipe', 'expert'), may hold values from 0.05 to 1
- west_affinity: float32 [4, 4096, 8], P('pipe', 'expert'), may hold values from 0.05 to 1
- norm_gain: float32 [4, 7168], P('pipe'), may hold values from 0.25 to 1.75
- w_gate: bfloat16 [4, 7168, 8192], P('pipe', None, 'expert'), may hold values from -0.0625 to 0.0625
- w_up: bfloat16 [4, 7168, 8192], P('pipe', None, 'expert'), may hold values from -0.0625 to 0.0625
- w_down: bfloat16 [4, 8192, 7168], P('pipe', 'expert'), may hold values from -0.1875 to 0.1875
- scales: int32 [4, 8, 56], P('pipe'), may hold values from -1 to 1
Outputs:
- east_out: bfloat16 [4, 4096, 7168], P('pipe', 'expert')
- west_out: bfloat16 [4, 4096, 7168], P('pipe', 'expert')
Inputs may be any that keep to these rules, and one draw needn't show every extreme that they name: `east_routes`: the 8 experts of a token differ. Among the 64 rows of one device, no expert is named more than 4 times, a bound that some block reaches. `west_routes`: the 8 experts of a token differ. Among the 64 rows of one device, no expert is named more than 4 times, a bound that some block reaches.
All inputs are finite; a program needn't handle non-finite values.
Results may differ from a plain program's by a relative error of at most 0.0071.
Values may be sent and summed in bfloat16 or wider, within the bound.
A program may use at most 128 MiB of HBM per device.

v0:
```python
import jax
import jax.numpy as jnp
from jax import lax
from jax.sharding import PartitionSpec as P

D = 7168
SPLIT = 8
CAP = 4


route_scale = 2.5


def shifted(block, axis, distance):
    devices = range(lax.axis_size(axis))
    route = [((i - distance) % len(devices), i) for i in devices]
    return lax.ppermute(block, axis, route)


def normalize(tokens, gain):
    values = tokens.astype(jnp.float32)
    meansq = jnp.mean(values * values, axis=-1, keepdims=True)
    return (values * lax.rsqrt(meansq + 1e-06) * gain).astype(jnp.bfloat16)


def layer_pass(tokens, routes, affinity, gain, w_gate, w_up, w_down, scales):
    groups = lax.axis_size("expert")
    window = groups // SPLIT
    my_index = lax.axis_index("expert")
    normed = normalize(tokens, gain)
    expert_ids = jnp.arange(window, dtype=jnp.int32)
    matches = routes[:, :, None] == expert_ids[None, None, :]
    chosen = jnp.sum(matches.astype(jnp.int32), axis=1)
    shares = route_scale * affinity / jnp.sum(affinity, axis=1, keepdims=True)
    weights = jnp.sum(matches.astype(jnp.float32) * shares[:, :, None], axis=1)
    ranked = jnp.cumsum(chosen, axis=0) - 1
    slot_ids = jnp.arange(CAP, dtype=jnp.int32)
    select = (ranked.T[:, None, :] == slot_ids[None, :, None]) & (chosen.T[:, None, :] > 0)
    packed = jnp.einsum(
        "ect,td->ced", select.astype(jnp.bfloat16), normed, preferred_element_type=jnp.float32
    ).astype(jnp.bfloat16)
    copies = jnp.broadcast_to(packed[:, :, None, :], (CAP, window, SPLIT, D)).reshape(
        CAP, groups, D
    )
    gathered = lax.all_to_all(copies, "expert", split_axis=1, concat_axis=1, tiled=True)
    own_expert = my_index // SPLIT
    picker = (expert_ids == own_expert).astype(jnp.float32)
    exponents = jnp.sum(picker[:, None] * scales.astype(jnp.float32), axis=0)
    factor = jnp.repeat(jnp.exp2(exponents), 128).astype(jnp.bfloat16)
    scaled = gathered.reshape(CAP * groups, D) * factor
    gate_out = jnp.dot(scaled, w_gate, preferred_element_type=jnp.float32)
    up_out = jnp.dot(scaled, w_up, preferred_element_type=jnp.float32)
    hidden = (jax.nn.silu(gate_out) * up_out).astype(jnp.bfloat16)
    partial_value = (
        jnp.dot(hidden, w_down, preferred_element_type=jnp.float32)
        .astype(jnp.bfloat16)
        .reshape(CAP, groups, D)
    )
    returned = lax.all_to_all(partial_value, "expert", split_axis=1, concat_axis=1, tiled=True)
    summed = jnp.sum(returned.reshape(CAP, window, SPLIT, D).astype(jnp.float32), axis=2)
    spread = select.astype(jnp.float32) * weights.T[:, None, :]
    combined = jnp.einsum("ect,ced->td", spread, summed, precision=lax.Precision.HIGHEST)
    return combined.astype(jnp.bfloat16)


def body(
    east_prev,
    west_prev,
    east_routes,
    west_routes,
    east_affinity,
    west_affinity,
    norm_gain,
    w_gate,
    w_up,
    w_down,
    scales,
):
    east_in = shifted(east_prev, "pipe", 1)
    west_in = shifted(west_prev, "pipe", -1)
    east_out = layer_pass(
        east_in[0],
        east_routes[0],
        east_affinity[0],
        norm_gain[0],
        w_gate[0],
        w_up[0],
        w_down[0],
        scales[0],
    )
    west_out = layer_pass(
        west_in[0],
        west_routes[0],
        west_affinity[0],
        norm_gain[0],
        w_gate[0],
        w_up[0],
        w_down[0],
        scales[0],
    )
    return (east_out[None], west_out[None])


def solution(mesh):
    placed = (
        P("pipe", "expert", None),
        P("pipe", "expert", None),
        P("pipe", "expert", None),
        P("pipe", "expert", None),
        P("pipe", "expert", None),
        P("pipe", "expert", None),
        P("pipe", None),
        P("pipe", None, "expert"),
        P("pipe", None, "expert"),
        P("pipe", "expert", None),
        P("pipe", None, None),
    )
    return jax.shard_map(
        body,
        mesh=mesh,
        in_specs=placed,
        out_specs=(P("pipe", "expert", None), P("pipe", "expert", None)),
        check_vma=False,
    )
```

profile of v0, /device:TPU:1, one launch (start us, length us, event | category | flops | bytes accessed | tf_op | source)
XLA Modules:
  0.0 422.6 jit_solution(7564138410774243639)
XLA Ops:
  0.6 2.8 collective-permute-start
  4.4 9.7 %collective-permute-done = bf16[1,64,7168]{2,1,0:T(8,128)(2,1)S(1)} collective-permute-done((bf16[1,64,7168]{2,1,0:T(8,128)(2,1)}, bf16[1,64,7168]{2,1,0:T(8,128)(2,1)S(1)}, u32[]{:S(2)}, u32[]{:S(2)}) %collective-permute-start) | collective-permute-done | bytes 917536 | tf_op jit(solution)/shard_map/ppermute | solution.py:17
  15.9 2.9 broadcast_in_dim.10
  18.8 14.4 %all-to-all-start = ((bf16[4,64,7168]{2,0,1:T(4,128)(2,1)}), bf16[4,64,7168]{2,0,1:T(4,128)(2,1)}, u32[]{:S(2)}, u32[]{:S(2)}) async-start(bf16[4,64,7168]{2,0,1:T(4,128)(2,1)} %bitcast.111), calls=%async_computation | async-start | bytes 7340032 | tf_op jit(solution)/shard_map/all_to_all | solution.py:45
  35.3 30.1 %collective-permute-done.1 = bf16[1,64,7168]{2,1,0:T(8,128)(2,1)S(1)} collective-permute-done((bf16[1,64,7168]{2,1,0:T(8,128)(2,1)}, bf16[1,64,7168]{2,1,0:T(8,128)(2,1)S(1)}, u32[]{:S(2)}, u32[]{:S(2)}) %collective-permute-start.1) | collective-permute-done | bytes 917536 | tf_op jit(solution)/shard_map/ppermute | solution.py:17
  66.5 48.5 %all-to-all-done = bf16[4,64,7168]{2,0,1:T(4,128)(2,1)} async-done(((bf16[4,64,7168]{2,0,1:T(4,128)(2,1)}), bf16[4,64,7168]{2,0,1:T(4,128)(2,1)}, u32[]{:S(2)}, u32[]{:S(2)}) %all-to-all-start) | async-done | bytes 3670048 | tf_op jit(solution)/shard_map/all_to_all | solution.py:45
  115.0 2.9 broadcast_in_dim.13
  117.9 9.6 %all-to-all-start.2 = ((bf16[4,64,7168]{2,0,1:T(4,128)(2,1)}), bf16[4,64,7168]{2,0,1:T(4,128)(2,1)}, u32[]{:S(2)}, u32[]{:S(2)}) async-start(bf16[4,64,7168]{2,0,1:T(4,128)(2,1)} %bitcast.110), calls=%async_computation.2 | async-start | bytes 7340032 | tf_op jit(solution)/shard_map/all_to_all | solution.py:45
  127.7 80.2 %all-to-all-done.2 = bf16[4,64,7168]{2,0,1:T(4,128)(2,1)} async-done(((bf16[4,64,7168]{2,0,1:T(4,128)(2,1)}), bf16[4,64,7168]{2,0,1:T(4,128)(2,1)}, u32[]{:S(2)}, u32[]{:S(2)}) %all-to-all-start.2) | async-done | bytes 3670048 | tf_op jit(solution)/shard_map/all_to_all | solution.py:45
  207.9 9.0 %copy_multiply_fusion = (bf16[4,64,7168]{2,1,0:T(8,128)(2,1)S(1)}, bf16[4,64,7168]{2,1,0:T(8,128)(2,1)}) fusion(bf16[4,64,7168]{2,0,1:T(4,128)(2,1)} %all-to-all-done.2, bf16[7168]{0:T(1024)(128)(2,1)S(1)} %broadcast_bitcast_fusion, bf16[4,64,7168]{2,0,1:T(4,128)(2,1)} %all-to-all-done), kind=kLoop, calls=%fused_computation.14 | loop fusion | flops 3670016 | bytes 14694400 | tf_op jit(solution)/shard_map/mul | solution.py:50
  216.9 1.9 copy-done.1
  219.9 6.6 %convolution_convert_fusion = bf16[256,7168]{1,0:T(8,128)(2,1)} fusion(bf16[1,128,7168]{2,1,0:T(8,128)(2,1)S(1)} %copy-done, bf16[256,7168]{1,0:T(8,128)(2,1)} %bitcast.109, bf16[1,7168,128]{2,1,0:T(8,128)(2,1)} %param.19, f32[256,128]{1,0:T(8,128)S(1)} %fusion.18), kind=kOutput, calls=%fused_computation | convolution fusion | flops 941555712 | bytes 11141120 | tf_op jit(solution)/shard_map/dot_general | solution.py:55
  226.5 6.8 %copy.73 = bf16[4,64,7168]{2,0,1:T(4,128)(2,1)} copy(bf16[4,64,7168]{2,1,0:T(8,128)(2,1)} %bitcast.112) | data formatting | bytes 7340032 | tf_op jit(solution)/shard_map/reshape | solution.py:57
  233.3 10.9 %all-to-all-start.3 = ((bf16[4,64,7168]{2,0,1:T(4,128)(2,1)}), bf16[4,64,7168]{2,0,1:T(4,128)(2,1)}, u32[]{:S(2)}, u32[]{:S(2)}) async-start(bf16[4,64,7168]{2,0,1:T(4,128)(2,1)} %copy.73), calls=%async_computation.3 | async-start | bytes 7340032 | tf_op jit(solution)/shard_map/all_to_all | solution.py:59
  244.1 3.7 fusion.20
  247.9 6.7 %convolution_convert_fusion.1 = bf16[256,7168]{1,0:T(8,128)(2,1)} fusion(bf16[1,128,7168]{2,1,0:T(8,128)(2,1)S(1)} %copy-done, bf16[256,7168]{1,0:T(8,128)(2,1)} %bitcast.107, bf16[1,7168,128]{2,1,0:T(8,128)(2,1)} %param.19, f32[256,128]{1,0:T(8,128)S(1)} %fusion.20), kind=kOutput, calls=%fused_computation.1 | convolution fusion | flops 941555712 | bytes 11141120 | tf_op jit(solution)/shard_map/dot_general | solution.py:55
  254.5 6.7 %copy.67 = bf16[4,64,7168]{2,0,1:T(4,128)(2,1)} copy(bf16[4,64,7168]{2,1,0:T(8,128)(2,1)} %bitcast.113) | data formatting | bytes 7340032 | tf_op jit(solution)/shard_map/reshape | solution.py:57
  261.2 63.5 %all-to-all-done.3 = bf16[4,64,7168]{2,0,1:T(4,128)(2,1)} async-done(((bf16[4,64,7168]{2,0,1:T(4,128)(2,1)}), bf16[4,64,7168]{2,0,1:T(4,128)(2,1)}, u32[]{:S(2)}, u32[]{:S(2)}) %all-to-all-start.3) | async-done | bytes 3670048 | tf_op jit(solution)/shard_map/all_to_all | solution.py:59
  324.7 10.6 %all-to-all-start.1 = ((bf16[4,64,7168]{2,0,1:T(4,128)(2,1)}), bf16[4,64,7168]{2,0,1:T(4,128)(2,1)}, u32[]{:S(2)}, u32[]{:S(2)}) async-start(bf16[4,64,7168]{2,0,1:T(4,128)(2,1)} %copy.67), calls=%async_computation.1 | async-start | bytes 7340032 | tf_op jit(solution)/shard_map/all_to_all | solution.py:59
  335.5 3.8 convert_reduce_fusion
  339.3 3.0 fusion.2
  342.3 73.6 %all-to-all-done.1 = bf16[4,64,7168]{2,0,1:T(4,128)(2,1)} async-done(((bf16[4,64,7168]{2,0,1:T(4,128)(2,1)}), bf16[4,64,7168]{2,0,1:T(4,128)(2,1)}, u32[]{:S(2)}, u32[]{:S(2)}) %all-to-all-start.1) | async-done | bytes 3670048 | tf_op jit(solution)/shard_map/all_to_all | solution.py:59
  415.8 3.8 convert_reduce_fusion.1
  419.7 3.0 fusion.3
  (49 shorter events, 7.3 us)
Async XLA Ops:
  0.6 219.3 %copy-start = (bf16[1,128,7168]{2,1,0:T(8,128)(2,1)S(1)}, bf16[1,128,7168]{2,1,0:T(8,128)(2,1)}, u32[]{:S(2)}) copy-start(bf16[1,128,7168]{2,1,0:T(8,128)(2,1)} %param.20) | copy-start | bytes 5505028
  0.6 13.4 %collective-permute-start = (bf16[1,64,7168]{2,1,0:T(8,128)(2,1)}, bf16[1,64,7168]{2,1,0:T(8,128)(2,1)S(1)}, u32[]{:S(2)}, u32[]{:S(2)}) collective-permute-start(bf16[1,64,7168]{2,1,0:T(8,128)(2,1)} %param.11), channel_id=1, source_target_pairs={{192,0},{0,64},{64,128},{128,192},{193,1},{1,65},{65,129},{129,193... | collective-permute-start | bytes 2752520 | tf_op jit(solution)/shard_map/ppermute | solution.py:17
  18.8 16.2 %copy-start.3 = (s32[1,64,8]{1,2,0:T(8,128)S(1)}, s32[1,64,8]{1,2,0:T(8,128)}, u32[]{:S(2)}) copy-start(s32[1,64,8]{1,2,0:T(8,128)} %param.14) | copy-start | bytes 6148
  18.8 46.9 %copy-start.8 = (f32[1,7168]{1,0:T(1,128)S(1)}, f32[1,7168]{1,0:T(1,128)}, u32[]{:S(2)}) copy-start(f32[1,7168]{1,0:T(1,128)} %param.17) | copy-start | bytes 86020
  18.8 96.2 %all-to-all-start = ((bf16[4,64,7168]{2,0,1:T(4,128)(2,1)}), bf16[4,64,7168]{2,0,1:T(4,128)(2,1)}, u32[]{:S(2)}, u32[]{:S(2)}) async-start(bf16[4,64,7168]{2,0,1:T(4,128)(2,1)} %bitcast.111), calls=%async_computation | async-start | bytes 7340032 | tf_op jit(solution)/shard_map/all_to_all | solution.py:45
  33.2 32.2 %collective-permute-start.1 = (bf16[1,64,7168]{2,1,0:T(8,128)(2,1)}, bf16[1,64,7168]{2,1,0:T(8,128)(2,1)S(1)}, u32[]{:S(2)}, u32[]{:S(2)}) collective-permute-start(bf16[1,64,7168]{2,1,0:T(8,128)(2,1)} %param.12), channel_id=1, source_target_pairs={{64,0},{128,64},{192,128},{0,192},{65,1},{129,65},{193,129},{1,193... | collective-permute-start | bytes 2752520 | tf_op jit(solution)/shard_map/ppermute | solution.py:17
  117.9 9.7 %copy-start.7 = (s32[1,8,56]{2,1,0:T(8,128)S(1)}, s32[1,8,56]{2,1,0:T(8,128)}, u32[]{:S(2)}) copy-start(s32[1,8,56]{2,1,0:T(8,128)} %param.21) | copy-start | bytes 5380
  117.9 90.0 %all-to-all-start.2 = ((bf16[4,64,7168]{2,0,1:T(4,128)(2,1)}), bf16[4,64,7168]{2,0,1:T(4,128)(2,1)}, u32[]{:S(2)}, u32[]{:S(2)}) async-start(bf16[4,64,7168]{2,0,1:T(4,128)(2,1)} %bitcast.110), calls=%async_computation.2 | async-start | bytes 7340032 | tf_op jit(solution)/shard_map/all_to_all | solution.py:45
  207.9 10.9 %copy-start.2 = (bf16[1,7168,128]{2,1,0:T(8,128)(2,1)S(1)}, bf16[1,7168,128]{2,1,0:T(8,128)(2,1)}, u32[]{:S(2)}) copy-start(bf16[1,7168,128]{2,1,0:T(8,128)(2,1)} %param.18) | copy-start | bytes 5505028
  216.9 1.9 copy-start.1
  233.3 91.5 %all-to-all-start.3 = ((bf16[4,64,7168]{2,0,1:T(4,128)(2,1)}), bf16[4,64,7168]{2,0,1:T(4,128)(2,1)}, u32[]{:S(2)}, u32[]{:S(2)}) async-start(bf16[4,64,7168]{2,0,1:T(4,128)(2,1)} %copy.73), calls=%async_computation.3 | async-start | bytes 7340032 | tf_op jit(solution)/shard_map/all_to_all | solution.py:59
  261.2 74.1 %copy-start.5 = (f32[1,64,8]{1,2,0:T(8,128)S(1)}, f32[1,64,8]{1,2,0:T(8,128)}, u32[]{:S(2)}) copy-start(f32[1,64,8]{1,2,0:T(8,128)} %param.16) | copy-start | bytes 6148
  261.2 74.2 %copy-start.6 = (f32[1,64,8]{1,2,0:T(8,128)S(1)}, f32[1,64,8]{1,2,0:T(8,128)}, u32[]{:S(2)}) copy-start(f32[1,64,8]{1,2,0:T(8,128)} %param.15) | copy-start | bytes 6148
  261.2 74.2 %copy-start.4 = (s32[1,64,8]{1,2,0:T(8,128)S(1)}, s32[1,64,8]{1,2,0:T(8,128)}, u32[]{:S(2)}) copy-start(s32[1,64,8]{1,2,0:T(8,128)} %param.13) | copy-start | bytes 6148
  324.7 91.1 %all-to-all-start.1 = ((bf16[4,64,7168]{2,0,1:T(4,128)(2,1)}), bf16[4,64,7168]{2,0,1:T(4,128)(2,1)}, u32[]{:S(2)}, u32[]{:S(2)}) async-start(bf16[4,64,7168]{2,0,1:T(4,128)(2,1)} %copy.67), calls=%async_computation.1 | async-start | bytes 7340032 | tf_op jit(solution)/shard_map/all_to_all | solution.py:59
where the time goes:
time: 426 us; the launch traced here: 423 us
  waiting for transfers between devices  306 us (72%)
  starting transfers between devices  50.1 us (12%)
  matrix products  25.6 us (6%)
  local copies, waits for them, and re-layouts  22.3 us (5%)
  other arithmetic  18.3 us (4%)
    all_to_all x2, waiting for transfers between devices, layer_pass(): lax.all_to_all(partial_value, 'expert', split_axis=1, concat_axis=1, tile...  137 us
    all_to_all x2, waiting for transfers between devices, layer_pass(): lax.all_to_all(copies, 'expert', split_axis=1, concat_axis=1, tiled=True)  129 us
    ppermute x2, waiting for transfers between devices, shifted(): return lax.ppermute(block, axis, route)  39.8 us
    all_to_all x2, starting transfers between devices, layer_pass(): lax.all_to_all(copies, 'expert', split_axis=1, concat_axis=1, tiled=True)  24 us
    all_to_all x2, starting transfers between devices, layer_pass(): lax.all_to_all(partial_value, 'expert', split_axis=1, concat_axis=1, tile...  21.5 us
    reshape x2, local copies, waits for them, and re-layouts, layer_pass(): partial_value = jnp.dot(hidden, w_down, preferred_element_type=jnp.float3...  13.4 us
    dot_general x2, matrix products, layer_pass(): jnp.dot(hidden, w_down, preferred_element_type=jnp.float32)  13.3 us
    mul x1, other arithmetic, layer_pass(): scaled = gathered.reshape(CAP * groups, D) * factor  8.96 us
  transfers between devices with their start and end apart: 6, of which 6 were waited for; matrix products, arithmetic and copies ran while one was open for 6% of the time, Pallas kernels for 0%

commit v1 on v0

v1 whole, which is shorter than its diff:
```python
import functools
import jax
import jax.numpy as jnp
from jax import lax
from jax.experimental import pallas as pl
from jax.experimental.pallas import tpu as pltpu
from jax.sharding import PartitionSpec as P

CAP = 4
NX, NY = 4, 2
NJ = NX * NY
NCH = 4
F32, BF16, I32 = jnp.float32, jnp.bfloat16, jnp.int32
MESH = pl.DeviceIdType.MESH
route_scale = 2.5


def cut(total, num, den):
    return (total * num // den) // 128 * 128


def kernel(
    np_, nz, d, tok, nf,
    xe, xw, rte, rtw, afe, afw, gain, wg, wu, wd, scales,
    oute, outw,
    X, RP, RR, AP, W, WD, GS, T1, T2, PK, Q, G, H, O, B, C, F, SP, OUT,
    s_loc, s_out, s_rt, r_rt, s_wd, r_wd, s_a, r_a, s_g, r_g, s_h, r_h, s_b, r_b, s_f, r_f,
):
    oc = d // NJ
    mr = nz * NJ * 2
    blk = 2 * nz
    ca = cut(d, 5, 9)
    qa = max(cut(d, 2, 9), 128)
    p = lax.axis_index("pipe")
    e = lax.axis_index("expert")
    z = e // NJ
    j = e % NJ
    y = j // NX
    x = j % NX
    base = z * NJ
    xr = (x + 1) % NX
    xl = (x + NX - 1) % NX
    x2 = (x + 2) % NX
    yo = 1 - y
    dev_r = (p, base + y * NX + xr)
    dev_l = (p, base + y * NX + xl)
    dev_y = (p, base + yo * NX + x)
    pn = (p + 1) % np_
    pp = (p + np_ - 1) % np_

    def rc(src, dst, ss, rs, dev):
        return pltpu.make_async_remote_copy(
            src_ref=src, dst_ref=dst, send_sem=ss, recv_sem=rs, device_id=dev, device_id_type=MESH
        )

    def drain(ref, sem):
        pltpu.make_async_copy(ref, ref, sem).wait()

    def ocol(o):
        return pl.ds(pl.multiple_of(o * oc, 128), oc)

    local = [
        pltpu.make_async_copy(xe, X.at[0], s_loc.at[0]),
        pltpu.make_async_copy(xw, X.at[1], s_loc.at[1]),
        pltpu.make_async_copy(wg, W.at[:, pl.ds(0, nf)], s_loc.at[2]),
        pltpu.make_async_copy(wu, W.at[:, pl.ds(nf, nf)], s_loc.at[3]),
        pltpu.make_async_copy(
            wd.at[:, ocol(j)], WD.at[pl.ds(pl.multiple_of(j * nf, 128), nf)], s_loc.at[4]
        ),
    ]
    for c in local:
        c.start()

    bar = pltpu.get_barrier_semaphore()

    def greet_z(k, carry):
        zz = (z + k) % nz
        pl.semaphore_signal(bar, inc=1, device_id=(pn, zz * NJ + j), device_id_type=MESH)
        pl.semaphore_signal(bar, inc=1, device_id=(pp, zz * NJ + j), device_id_type=MESH)
        return carry

    lax.fori_loop(0, nz, greet_z, 0)

    def greet_own(k, carry):
        pl.semaphore_signal(
            bar, inc=1, device_id=(p, (z + k) % nz * NJ + j), device_id_type=MESH
        )
        return carry

    lax.fori_loop(1, nz, greet_own, 0)

    def greet_j(k, carry):
        pl.semaphore_signal(bar, inc=1, device_id=(p, base + (j + k) % NJ), device_id_type=MESH)
        return carry

    lax.fori_loop(1, NJ, greet_j, 0)

    RP[...] = jnp.full(RP.shape, -1, I32)
    RP[0, :, 0:tok] = rte[...]
    RP[1, :, 0:tok] = rtw[...]
    AP[...] = jnp.full(AP.shape, 1.0, F32)
    AP[0, :, 0:tok] = afe[...]
    AP[1, :, 0:tok] = afw[...]

    pl.semaphore_wait(bar, 2 * nz + (nz - 1) + (NJ - 1))

    rt_e = rc(RP.at[0], RR.at[0], s_rt.at[0], r_rt.at[0], (pp, e))
    rt_w = rc(RP.at[1], RR.at[1], s_rt.at[1], r_rt.at[1], (pn, e))
    rt_e.start()
    rt_w.start()

    def send_wd(k, carry):
        t = (j + k) % NJ
        rc(
            wd.at[:, ocol(t)],
            WD.at[pl.ds(pl.multiple_of(j * nf, 128), nf)],
            s_wd.at[0],
            r_wd.at[0],
            (p, base + t),
        ).start()
        return carry

    lax.fori_loop(1, NJ, send_wd, 0)

    def iot(shape, dim):
        return lax.broadcasted_iota(I32, shape, dim)

    r_ = iot((mr, mr), 0)
    c_ = iot((mr, mr), 1)
    hit = (
        (r_ // blk == (c_ // 2) % NJ) & ((r_ // 2) % nz == c_ // (2 * NJ)) & (r_ % 2 == c_ % 2)
    )
    T1[...] = hit.astype(F32).astype(BF16)
    hit2 = (
        (c_ // blk == (r_ // 2) % NJ) & ((c_ // 2) % nz == r_ // (2 * NJ)) & (r_ % 2 == c_ % 2)
    )
    T2[...] = hit2.astype(F32).astype(BF16)

    def gain_block(k, carry):
        s = scales[z, k]
        f = jnp.where(s > 0, 2.0, jnp.where(s < 0, 0.5, 1.0)).astype(F32)
        cols = pl.ds(pl.multiple_of(k * 128, 128), 128)
        GS[:, cols] = gain[:, cols] * f
        return carry

    lax.fori_loop(0, d // 128, gain_block, 0)

    lanes = RP.shape[2]
    row = iot((mr, lanes), 0)
    zrow = row // (2 * NJ)
    orow = (row // 2) % NJ
    crow = row % 2
    before = (iot((lanes, lanes), 0) < iot((lanes, lanes), 1)).astype(F32).astype(BF16)

    def slots(rt):
        chosen = jnp.zeros((mr, lanes), F32)
        for k in range(rt.shape[0]):
            chosen = chosen + jnp.where(rt[k : k + 1, :] == zrow, 1.0, 0.0)
        rank = jnp.dot(chosen.astype(BF16), before, preferred_element_type=F32)
        return chosen, rank.astype(I32)

    local[0].wait()
    local[1].wait()
    rt_e.wait_recv()
    rt_w.wait_recv()

    def stage_a(c):
        m, k = c // 2, c % 2
        chosen, rank = slots(RR[m])
        pick = jnp.where((chosen > 0.0) & (rank == 2 * k + crow), 1.0, 0.0)
        acc = jnp.zeros((mr, oc), F32)
        for o in range(NJ):
            part = jnp.where(orow == o, pick, 0.0).astype(BF16)[:, 0:tok]
            acc = acc + jnp.dot(part, X[m, :, o * oc : (o + 1) * oc], preferred_element_type=F32)
        PK[c] = acc.astype(BF16)
        to = (p + 1 + m * (np_ - 2)) % np_

        def send(i, carry):
            t = (z + i) % nz
            rc(
                PK.at[c, pl.ds(pl.multiple_of(t * 2 * NJ, 16), 2 * NJ)],
                Q.at[c, pl.ds(pl.multiple_of(z * 2 * NJ, 16), 2 * NJ)],
                s_a.at[c],
                r_a.at[c],
                (to, t * NJ + j),
            ).start()
            return carry

        lax.fori_loop(0, nz, send, 0)

    def blk_of(c, yy, xx, lo, hi):
        return G.at[c, yy * NX + xx, :, pl.ds(lo, hi - lo)]

    def msg(c, n, yy, xx, lo, hi, dev):
        ref = blk_of(c, yy, xx, lo, hi)
        return rc(ref, ref, s_g.at[c, n], r_g.at[c, n], dev)

    def level0(c):
        return (
            msg(c, 0, y, x, 0, d, dev_r),
            msg(c, 1, y, x, 0, d, dev_l),
            msg(c, 2, y, x, 0, d, dev_y),
        )

    def level1(c):
        return (
            msg(c, 3, y, xl, 0, ca, dev_r),
            msg(c, 4, y, xr, ca, d, dev_l),
            msg(c, 5, y, xl, ca, d, dev_y),
            msg(c, 6, y, xr, ca, d, dev_y),
            msg(c, 7, yo, x, 0, ca, dev_r),
            msg(c, 8, yo, x, 0, ca, dev_l),
        )

    def level2(c):
        return (
            msg(c, 9, y, x2, ca, d, dev_y),
            msg(c, 10, yo, xl, 0, qa, dev_r),
            msg(c, 11, yo, xr, qa, ca, dev_l),
        )

    def stage_b(c):
        drain(Q.at[c], r_a.at[c])
        u = jnp.dot(T1[...], Q[c], preferred_element_type=F32)
        sq = jnp.zeros((blk, 1), F32)
        for o in range(NJ):
            v = u[o * blk : (o + 1) * blk]
            sq = sq + jnp.sum(v * v, axis=1, keepdims=True)
        inv = lax.rsqrt(sq / d + 1e-6)
        for o in range(NJ):
            v = u[o * blk : (o + 1) * blk]
            G[c, j, :, o * oc : (o + 1) * oc] = (v * inv * GS[:, o * oc : (o + 1) * oc]).astype(BF16)
        for s in level0(c):
            s.start()

    def stage_l1(c):
        a, b, w = level0(c)
        m3, m4, m5, m6, m7, m8 = level1(c)
        a.wait_recv()
        m3.start()
        m5.start()
        b.wait_recv()
        m4.start()
        m6.start()
        w.wait_recv()
        m7.start()
        m8.start()

    def stage_l2(c):
        _, m4, _, _, m7, m8 = level1(c)
        m9, m10, m11 = level2(c)
        m4.wait_recv()
        m9.start()
        m7.wait_recv()
        m10.start()
        m8.wait_recv()
        m11.start()

    def stage_d(c):
        m3, _, m5, m6, _, _ = level1(c)
        for s in (m3, m5, m6) + level2(c):
            s.wait_recv()
        kb = d // 7 if d % (7 * 128) == 0 else 128

        def step(i, acc):
            cols = pl.ds(pl.multiple_of(i * kb, 128), kb)
            rows = G[c, :, :, cols].reshape(NJ * blk, kb)
            return acc + jnp.dot(rows, W[cols, :], preferred_element_type=F32)

        acc = lax.fori_loop(0, d // kb, step, jnp.zeros((NJ * blk, 2 * nf), F32))
        gate, up = acc[:, 0:nf], acc[:, nf : 2 * nf]
        H[c, j] = (gate / (1.0 + jnp.exp(-gate)) * up).astype(BF16)

        def send(i, carry):
            t = (j + i) % NJ
            rc(H.at[c, j], H.at[c, j], s_h.at[c], r_h.at[c], (p, base + t)).start()
            return carry

        lax.fori_loop(1, NJ, send, 0)

    def stage_e(c):
        drain(H.at[c, pl.ds(0, NJ - 1)], r_h.at[c])
        hid = jnp.concatenate([H[c, i] for i in range(NJ)], axis=1)
        O[c] = jnp.dot(hid, WD[...], preferred_element_type=F32).astype(BF16)
        own = pl.ds(pl.multiple_of(j * blk, blk), blk)
        B[c, own] = O[c, own]

        def send(i, carry):
            t = (j + i) % NJ
            rc(
                O.at[c, pl.ds(pl.multiple_of(t * blk, blk), blk)],
                B.at[c, own],
                s_b.at[c],
                r_b.at[c],
                (p, base + t),
            ).start()
            return carry

        lax.fori_loop(1, NJ, send, 0)

    def stage_f(c):
        drain(B.at[c, pl.ds(0, (NJ - 1) * blk)], r_b.at[c])
        C[c] = jnp.dot(T2[...], B[c], preferred_element_type=F32).astype(BF16)
        own = pl.ds(pl.multiple_of(z * 2 * NJ, 16), 2 * NJ)
        F[c, own] = C[c, own]

        def send(i, carry):
            t = (z + i) % nz
            rc(
                C.at[c, pl.ds(pl.multiple_of(t * 2 * NJ, 16), 2 * NJ)],
                F.at[c, own],
                s_f.at[c],
                r_f.at[c],
                (p, t * NJ + j),
            ).start()
            return carry

        lax.fori_loop(1, nz, send, 0)

    def spread(m):
        rt = RP[m]
        af = AP[m]
        share = route_scale * af / jnp.sum(af, axis=0, keepdims=True)
        weight = jnp.zeros((mr, lanes), F32)
        for k in range(rt.shape[0]):
            weight = weight + jnp.where(rt[k : k + 1, :] == zrow, share[k : k + 1, :], 0.0)
        chosen, rank = slots(rt)
        olane = (iot((tok, mr), 1) // 2) % NJ
        for k in range(2):
            s = jnp.where((chosen > 0.0) & (rank == 2 * k + crow), weight, 0.0)
            s = jnp.transpose(s)[0:tok]
            hi = s.astype(BF16).astype(F32)
            lo = s - hi
            for h, v in ((0, hi), (1, lo)):
                for o in range(NJ):
                    SP[m, h, o * tok : (o + 1) * tok, k * mr : (k + 1) * mr] = jnp.where(
                        olane == o, v, 0.0
                    ).astype(BF16)

    def stage_g(m):
        for k in range(2):
            drain(F.at[2 * m + k, pl.ds(0, (nz - 1) * 2 * NJ)], r_f.at[2 * m + k])
        rows = F[pl.ds(2 * m, 2)].reshape(2 * mr, oc)
        res = jnp.dot(SP[m, 0], rows, preferred_element_type=F32)
        res = res + jnp.dot(SP[m, 1], rows, preferred_element_type=F32)
        for o in range(NJ):
            OUT[m, :, o * oc : (o + 1) * oc] = res[o * tok : (o + 1) * tok].astype(BF16)

    def pack_loop(c, carry):
        stage_a(c)
        return carry

    lax.fori_loop(0, NCH, pack_loop, 0)
    spread(0)
    spread(1)

    def main(it, carry):
        def when(lag, f):
            c = it - lag
            pl.when((c >= 0) & (c < NCH))(lambda: f(c))

        when(0, stage_b)
        when(1, stage_l1)
        when(2, stage_l2)

        @pl.when(it == 3)
        def _():
            local[2].wait()
            local[3].wait()
            local[4].wait()
            drain(WD.at[pl.ds(0, (NJ - 1) * nf)], r_wd.at[0])

        when(3, stage_d)
        when(4, stage_e)
        when(5, stage_f)

        @pl.when(it == 7)
        def _():
            stage_g(0)
            pltpu.make_async_copy(OUT.at[0], oute, s_out.at[0]).start()

        @pl.when(it == 9)
        def _():
            stage_g(1)
            pltpu.make_async_copy(OUT.at[1], outw, s_out.at[1]).start()

        return carry

    lax.fori_loop(0, 10, main, 0)

    rt_e.wait_send()
    rt_w.wait_send()
    drain(WD.at[pl.ds(0, (NJ - 1) * nf)], s_wd.at[0])

    def finish(c, carry):
        drain(PK.at[c], s_a.at[c])
        for s in level0(c) + level1(c) + level2(c):
            s.wait_send()
        drain(H.at[c, pl.ds(0, NJ - 1)], s_h.at[c])
        drain(O.at[c, pl.ds(0, (NJ - 1) * blk)], s_b.at[c])
        drain(C.at[c, pl.ds(0, (nz - 1) * 2 * NJ)], s_f.at[c])
        return carry

    lax.fori_loop(0, NCH, finish, 0)
    pltpu.make_async_copy(OUT.at[0], oute, s_out.at[0]).wait()
    pltpu.make_async_copy(OUT.at[1], outw, s_out.at[1]).wait()


def body(mesh_shape, xe, xw, rte, rtw, afe, afw, gain, wg, wu, wd, scales):
    np_, ne = mesh_shape
    nz = ne // NJ
    _, tok, d = xe.shape
    nf = wg.shape[2]
    oc = d // NJ
    mr = nz * NJ * 2
    blk = 2 * nz
    top = rte.shape[2]
    any_, vm = pl.BlockSpec(memory_space=pl.ANY), pl.BlockSpec(memory_space=pltpu.VMEM)
    dma = pltpu.SemaphoreType.DMA
    flops = 2 * NCH * NJ * blk * d * 3 * nf
    moved = 2 * 2 * (4 * tok * d + 3 * d * nf)
    outs = pl.pallas_call(
        functools.partial(kernel, np_, nz, d, tok, nf),
        out_shape=[jax.ShapeDtypeStruct((tok, d), BF16)] * 2,
        in_specs=[any_, any_, vm, vm, vm, vm, vm, any_, any_, any_]
        + [pl.BlockSpec(memory_space=pltpu.SMEM)],
        out_specs=[any_, any_],
        scratch_shapes=[
            pltpu.VMEM((2, tok, d), BF16),
            pltpu.VMEM((2, top, 128), I32),
            pltpu.VMEM((2, top, 128), I32),
            pltpu.VMEM((2, top, 128), F32),
            pltpu.VMEM((d, 2 * nf), BF16),
            pltpu.VMEM((NJ * nf, oc), BF16),
            pltpu.VMEM((1, d), F32),
            pltpu.VMEM((mr, mr), BF16),
            pltpu.VMEM((mr, mr), BF16),
            pltpu.VMEM((NCH, mr, oc), BF16),
            pltpu.VMEM((NCH, mr, oc), BF16),
            pltpu.VMEM((NCH, NJ, blk, d), BF16),
            pltpu.VMEM((NCH, NJ, NJ * blk, nf), BF16),
            pltpu.VMEM((NCH, NJ * blk, oc), BF16),
            pltpu.VMEM((NCH, NJ * blk, oc), BF16),
            pltpu.VMEM((NCH, mr, oc), BF16),
            pltpu.VMEM((NCH, mr, oc), BF16),
            pltpu.VMEM((2, 2, NJ * tok, 2 * mr), BF16),
            pltpu.VMEM((2, tok, d), BF16),
            dma((5,)),
            dma((2,)),
            dma((2,)),
            dma((2,)),
            dma((1,)),
            dma((1,)),
            dma((NCH,)),
            dma((NCH,)),
            dma((NCH, 12)),
            dma((NCH, 12)),
            dma((NCH,)),
            dma((NCH,)),
            dma((NCH,)),
            dma((NCH,)),
            dma((NCH,)),
            dma((NCH,)),
        ],
        compiler_params=pltpu.CompilerParams(
            collective_id=0, has_side_effects=True, vmem_limit_bytes=48 * 2**20
        ),
        cost_estimate=pl.CostEstimate(flops=flops, bytes_accessed=moved, transcendentals=0),
    )(
        xe[0], xw[0], rte[0].T, rtw[0].T, afe[0].T, afw[0].T, gain,
        wg[0], wu[0], wd[0], scales[0],
    )
    return outs[0][None], outs[1][None]


def solution(mesh):
    tokens = P("pipe", "expert", None)
    placed = (tokens,) * 6 + (
        P("pipe", None),
        P("pipe", None, "expert"),
        P("pipe", None, "expert"),
        P("pipe", "expert", None),
        P("pipe", None, None),
    )
    return jax.shard_map(
        functools.partial(body, (mesh.shape["pipe"], mesh.shape["expert"])),
        mesh=mesh,
        in_specs=placed,
        out_specs=(tokens, tokens),
        check_vma=False,
    )
```

time: 426 us -> 138 us (0.32)
  waiting for transfers between devices: 306 us -> 0 us
  Pallas kernels: 0 us -> 127 us
  starting transfers between devices: 50.1 us -> 0 us
  matrix products: 25.6 us -> 0 us
  other arithmetic: 18.3 us -> 0 us
  local copies, waits for them, and re-layouts: 22.3 us -> 9.88 us
    all_to_all x4 -> x0, waiting for transfers between devices: 266 us -> none  [the longest x2 137 us: layer_pass(): lax.all_to_all(partial_value, 'expert', split_axis=1, concat_axis=1, tile...]
    pallas_call x0 -> x1, Pallas kernels: none -> 127 us  [body(): pl.pallas_call(functools.partial(kernel, np_, nz, d, tok, nf), out_shape=...]
    all_to_all x4 -> x0, starting transfers between devices: 45.5 us -> none  [the longest x2 24 us: layer_pass(): lax.all_to_all(copies, 'expert', split_axis=1, concat_axis=1, tiled=True)]
    ppermute x2 -> x0, waiting for transfers between devices: 39.8 us -> none  [shifted(): return lax.ppermute(block, axis, route)]
    dot_general x8 -> x0, matrix products: 25.6 us -> none  [the longest x2 13.3 us: layer_pass(): jnp.dot(hidden, w_down, preferred_element_type=jnp.float32)]
    reshape x2 -> x0, local copies, waits for them, and re-layouts: 13.4 us -> none  [layer_pass(): partial_value = jnp.dot(hidden, w_down, preferred_element_type=jnp.float3...]
    reduce_sum x11 -> x0, other arithmetic: 9.11 us -> none  [the longest x2 7.69 us: layer_pass(): jnp.sum(returned.reshape(CAP, window, SPLIT, D).astype(jnp.float32), axis=2)]
    mul x1 -> x0, other arithmetic: 8.96 us -> none  [layer_pass(): scaled = gathered.reshape(CAP * groups, D) * factor]
  transfers between devices with their start and end apart: 6 -> 0, of which waited for: 6 -> 0; matrix products, arithmetic and copies ran while one was open for 6% -> 0% of each run, Pallas kernels for 0% -> 0%
where the time goes in v1:
time: 138 us
  Pallas kernels  127 us (92%)
  local copies, waits for them, and re-layouts  9.88 us (7%)
    pallas_call x1, Pallas kernels, body(): pl.pallas_call(functools.partial(kernel, np_, nz, d, tok, nf), out_shape=...  127 us
    unnamed x20, local copies, waits for them, and re-layouts  9.88 us

profile of v1, /device:TPU:1, one launch (start us, length us, event | category | flops | bytes accessed | tf_op | source)
XLA Modules:
  0.0 137.6 jit_solution(895962137755461810)
XLA Ops:
  0.6 0.0 copy-start
  0.6 1.5 %copy-done = bf16[1,7168,128]{2,1,0:T(8,128)(2,1)S(1)} copy-done((bf16[1,7168,128]{2,1,0:T(8,128)(2,1)S(1)}, bf16[1,7168,128]{2,1,0:T(8,128)(2,1)}, u32[]{:S(2)}) %copy-start) | copy-done | bytes 1835032
  2.1 0.0 copy-start.1
  2.1 1.2 copy-done.1
  3.3 0.0 copy-start.2
  3.3 1.2 copy-done.2
  4.5 0.0 copy-start.3
  4.5 0.7 copy-done.3
  5.2 0.0 copy-start.4
  5.2 0.7 copy-done.4
  5.9 0.0 copy-start.5
  5.9 0.7 copy-done.5
  6.6 0.0 copy-start.6
  6.6 0.7 copy-done.6
  7.3 0.0 copy-start.7
  7.3 0.7 copy-done.7
  8.0 0.0 copy-start.8
  8.0 0.7 copy-done.8
  8.7 127.1 %shard_map.122 = (bf16[64,7168]{1,0:T(8,128)(2,1)S(1)}, bf16[64,7168]{1,0:T(8,128)(2,1)S(1)}) custom-call(bf16[64,7168]{1,0:T(8,128)(2,1)S(1)} %bitcast.23, bf16[64,7168]{1,0:T(8,128)(2,1)S(1)} %bitcast.24, s32[8,64]{1,0:T(8,128)S(1)} %bitcast.25, s32[8,64]{1,0:T(8,128)S(1)} %bitcast.26, f32[8,64]{1,0:T(8,128)S(1)} %bitcast.27, f32[8,64]{1,0:T(8,128)S(1)} %bitcast.28, ...), custom_call_target="tpu_custom_call" | custom-call | flops 2818572288 | bytes 18350080 | tf_op jit(solution)/shard_map/pallas_call | solution.py:422
  135.8 0.9 copy.15
  136.7 0.9 copy.16
Async XLA Ops:
  0.6 1.5 %copy-start = (bf16[1,7168,128]{2,1,0:T(8,128)(2,1)S(1)}, bf16[1,7168,128]{2,1,0:T(8,128)(2,1)}, u32[]{:S(2)}) copy-start(bf16[1,7168,128]{2,1,0:T(8,128)(2,1)} %param.18) | copy-start | bytes 5505028
  2.1 1.2 copy-start.1
  3.3 1.2 copy-start.2
  4.5 0.7 copy-start.3
  5.2 0.7 copy-start.4
  5.9 0.7 copy-start.5
  6.6 0.7 copy-start.6
  7.3 0.7 copy-start.7
  8.0 0.7 copy-start.8

commit v2 on v1

--- a/solution.py
+++ b/solution.py
@@ -23,12 +23,14 @@
     np_, nz, d, tok, nf,
     xe, xw, rte, rtw, afe, afw, gain, wg, wu, wd, scales,
     oute, outw,
-    X, RP, RR, AP, W, WD, GS, T1, T2, PK, Q, G, H, O, B, C, F, SP, OUT,
-    s_loc, s_out, s_rt, r_rt, s_wd, r_wd, s_a, r_a, s_g, r_g, s_h, r_h, s_b, r_b, s_f, r_f,
+    X, RP, RR, AP, W, WD, GS, T1, T2, PK, Q, G, H, OY, YR, PF, SR, B, C, F, SP, OUT,
+    s_loc, s_out, s_rt, r_rt, s_wd, r_wd, s_a, r_a, s_g, r_g, s_h, r_h, s_y, r_y, s_b, r_b, s_f, r_f,
 ):
     oc = d // NJ
+    qc = d // NX
     mr = nz * NJ * 2
     blk = 2 * nz
+    half = NX * blk
     ca = cut(d, 5, 9)
     qa = max(cut(d, 2, 9), 128)
     p = lax.axis_index("pipe")
@@ -56,8 +58,13 @@
     def drain(ref, sem):
         pltpu.make_async_copy(ref, ref, sem).wait()
 
-    def ocol(o):
-        return pl.ds(pl.multiple_of(o * oc, 128), oc)
+    def qcol(q):
+        return pl.ds(pl.multiple_of(q * qc, 128), qc)
+
+    def on_row(send):
+        for k in (1, 3, 2):
+            t = (x + k) % NX
+            send(t, (p, base + y * NX + t))
 
     local = [
         pltpu.make_async_copy(xe, X.at[0], s_loc.at[0]),
@@ -65,7 +72,7 @@
         pltpu.make_async_copy(wg, W.at[:, pl.ds(0, nf)], s_loc.at[2]),
         pltpu.make_async_copy(wu, W.at[:, pl.ds(nf, nf)], s_loc.at[3]),
         pltpu.make_async_copy(
-            wd.at[:, ocol(j)], WD.at[pl.ds(pl.multiple_of(j * nf, 128), nf)], s_loc.at[4]
+            wd.at[:, qcol(x)], WD.at[pl.ds(pl.multiple_of(x * nf, 128), nf)], s_loc.at[4]
         ),
     ]
     for c in local:
@@ -89,11 +96,11 @@
 
     lax.fori_loop(1, nz, greet_own, 0)
 
-    def greet_j(k, carry):
-        pl.semaphore_signal(bar, inc=1, device_id=(p, base + (j + k) % NJ), device_id_type=MESH)
-        return carry
-
-    lax.fori_loop(1, NJ, greet_j, 0)
+    def greet(t, dev):
+        pl.semaphore_signal(bar, inc=1, device_id=dev, device_id_type=MESH)
+
+    on_row(greet)
+    greet(x, dev_y)
 
     RP[...] = jnp.full(RP.shape, -1, I32)
     RP[0, :, 0:tok] = rte[...]
@@ -102,48 +109,26 @@
     AP[0, :, 0:tok] = afe[...]
     AP[1, :, 0:tok] = afw[...]
 
-    pl.semaphore_wait(bar, 2 * nz + (nz - 1) + (NJ - 1))
+    pl.semaphore_wait(bar, 2 * nz + (nz - 1) + NX)
 
     rt_e = rc(RP.at[0], RR.at[0], s_rt.at[0], r_rt.at[0], (pp, e))
     rt_w = rc(RP.at[1], RR.at[1], s_rt.at[1], r_rt.at[1], (pn, e))
     rt_e.start()
     rt_w.start()
 
-    def send_wd(k, carry):
-        t = (j + k) % NJ
+    def send_wd(t, dev):
         rc(
-            wd.at[:, ocol(t)],
-            WD.at[pl.ds(pl.multiple_of(j * nf, 128), nf)],
+            wd.at[:, qcol(t)],
+            WD.at[pl.ds(pl.multiple_of(x * nf, 128), nf)],
             s_wd.at[0],
             r_wd.at[0],
-            (p, base + t),
+            dev,
         ).start()
-        return carry
-
-    lax.fori_loop(1, NJ, send_wd, 0)
+
+    on_row(send_wd)
 
     def iot(shape, dim):
         return lax.broadcasted_iota(I32, shape, dim)
-
-    r_ = iot((mr, mr), 0)
-    c_ = iot((mr, mr), 1)
-    hit = (
-        (r_ // blk == (c_ // 2) % NJ) & ((r_ // 2) % nz == c_ // (2 * NJ)) & (r_ % 2 == c_ % 2)
-    )
-    T1[...] = hit.astype(F32).astype(BF16)
-    hit2 = (
-        (c_ // blk == (r_ // 2) % NJ) & ((c_ // 2) % nz == r_ // (2 * NJ)) & (r_ % 2 == c_ % 2)
-    )
-    T2[...] = hit2.astype(F32).astype(BF16)
-
-    def gain_block(k, carry):
-        s = scales[z, k]
-        f = jnp.where(s > 0, 2.0, jnp.where(s < 0, 0.5, 1.0)).astype(F32)
-        cols = pl.ds(pl.multiple_of(k * 128, 128), 128)
-        GS[:, cols] = gain[:, cols] * f
-        return carry
-
-    lax.fori_loop(0, d // 128, gain_block, 0)
 
     lanes = RP.shape[2]
     row = iot((mr, lanes), 0)
@@ -173,6 +158,9 @@
             part = jnp.where(orow == o, pick, 0.0).astype(BF16)[:, 0:tok]
             acc = acc + jnp.dot(part, X[m, :, o * oc : (o + 1) * oc], preferred_element_type=F32)
         PK[c] = acc.astype(BF16)
+
+    def send_a(c):
+        m = c // 2
         to = (p + 1 + m * (np_ - 2)) % np_
 
         def send(i, carry):
@@ -269,37 +257,55 @@
 
         acc = lax.fori_loop(0, d // kb, step, jnp.zeros((NJ * blk, 2 * nf), F32))
         gate, up = acc[:, 0:nf], acc[:, nf : 2 * nf]
-        H[c, j] = (gate / (1.0 + jnp.exp(-gate)) * up).astype(BF16)
-
-        def send(i, carry):
-            t = (j + i) % NJ
-            rc(H.at[c, j], H.at[c, j], s_h.at[c], r_h.at[c], (p, base + t)).start()
-            return carry
-
-        lax.fori_loop(1, NJ, send, 0)
+        H[c, x] = (gate / (1.0 + jnp.exp(-gate)) * up).astype(BF16)
+
+        def send(t, dev):
+            rc(H.at[c, x], H.at[c, x], s_h.at[c], r_h.at[c], dev).start()
+
+        on_row(send)
+
+    def to_y(c):
+        return rc(OY.at[c], YR.at[c], s_y.at[c], r_y.at[c], dev_y)
 
     def stage_e(c):
-        drain(H.at[c, pl.ds(0, NJ - 1)], r_h.at[c])
-        hid = jnp.concatenate([H[c, i] for i in range(NJ)], axis=1)
-        O[c] = jnp.dot(hid, WD[...], preferred_element_type=F32).astype(BF16)
-        own = pl.ds(pl.multiple_of(j * blk, blk), blk)
-        B[c, own] = O[c, own]
-
-        def send(i, carry):
-            t = (j + i) % NJ
-            rc(
-                O.at[c, pl.ds(pl.multiple_of(t * blk, blk), blk)],
-                B.at[c, own],
-                s_b.at[c],
-                r_b.at[c],
-                (p, base + t),
-            ).start()
-            return carry
-
-        lax.fori_loop(1, NJ, send, 0)
+        drain(H.at[c, pl.ds(0, NX - 1)], r_h.at[c])
+
+        def down(yy):
+            rows = pl.ds(pl.multiple_of(yy * half, half), half)
+            hid = jnp.concatenate([H[c, i, rows] for i in range(NX)], axis=1)
+            return jnp.dot(hid, WD[...], preferred_element_type=F32)
+
+        OY[c] = down(yo).astype(BF16)
+        to_y(c).start()
+        PF[c] = down(y)
+
+    def stage_s(c):
+        to_y(c).wait_recv()
+        SR[c] = (PF[c] + YR[c].astype(F32)).astype(BF16)
+
+        def octant(h):
+            return pl.ds(pl.multiple_of((2 * x + h) * blk, blk), blk)
+
+        def rows(t):
+            return pl.ds(pl.multiple_of(t * blk, blk), blk)
+
+        for h in range(2):
+            B[c, octant(h)] = SR[c, rows(x), h * oc : (h + 1) * oc]
+
+        def send(t, dev):
+            for h in range(2):
+                rc(
+                    SR.at[c, rows(t), pl.ds(h * oc, oc)],
+                    B.at[c, octant(h)],
+                    s_b.at[c],
+                    r_b.at[c],
+                    dev,
+                ).start()
+
+        on_row(send)
 
     def stage_f(c):
-        drain(B.at[c, pl.ds(0, (NJ - 1) * blk)], r_b.at[c])
+        drain(B.at[c, pl.ds(0, 2 * (NX - 1) * blk)], r_b.at[c])
         C[c] = jnp.dot(T2[...], B[c], preferred_element_type=F32).astype(BF16)
         own = pl.ds(pl.multiple_of(z * 2 * NJ, 16), 2 * NJ)
         F[c, own] = C[c, own]
@@ -348,9 +354,30 @@
 
     def pack_loop(c, carry):
         stage_a(c)
+        pl.when(c == 0)(lambda: send_a(c))
         return carry
 
     lax.fori_loop(0, NCH, pack_loop, 0)
+    r_ = iot((mr, mr), 0)
+    c_ = iot((mr, mr), 1)
+    hit = (
+        (r_ // blk == (c_ // 2) % NJ) & ((r_ // 2) % nz == c_ // (2 * NJ)) & (r_ % 2 == c_ % 2)
+    )
+    T1[...] = hit.astype(F32).astype(BF16)
+    hit2 = (
+        (c_ // blk == (r_ // 2) % NJ) & ((c_ // 2) % nz == r_ // (2 * NJ)) & (r_ % 2 == c_ % 2)
+    )
+    T2[...] = hit2.astype(F32).astype(BF16)
+
+    def gain_block(k, carry):
+        s = scales[z, k]
+        f = jnp.where(s > 0, 2.0, jnp.where(s < 0, 0.5, 1.0)).astype(F32)
+        cols = pl.ds(pl.multiple_of(k * 128, 128), 128)
+        GS[:, cols] = gain[:, cols] * f
+        return carry
+
+    lax.fori_loop(0, d // 128, gain_block, 0)
+
     spread(0)
     spread(1)
 
@@ -359,6 +386,11 @@
             c = it - lag
             pl.when((c >= 0) & (c < NCH))(lambda: f(c))
 
+        def next_a(c):
+            drain(PK.at[c], s_a.at[c])
+            send_a(c + 1)
+
+        pl.when(it < NCH - 1)(lambda: next_a(it))
         when(0, stage_b)
         when(1, stage_l1)
         when(2, stage_l2)
@@ -368,40 +400,42 @@
             local[2].wait()
             local[3].wait()
             local[4].wait()
-            drain(WD.at[pl.ds(0, (NJ - 1) * nf)], r_wd.at[0])
+            drain(WD.at[pl.ds(0, (NX - 1) * nf)], r_wd.at[0])
 
         when(3, stage_d)
         when(4, stage_e)
-        when(5, stage_f)
-
-        @pl.when(it == 7)
+        when(5, stage_s)
+        when(6, stage_f)
+
+        @pl.when(it == 8)
         def _():
             stage_g(0)
             pltpu.make_async_copy(OUT.at[0], oute, s_out.at[0]).start()
 
-        @pl.when(it == 9)
+        @pl.when(it == 10)
         def _():
             stage_g(1)
             pltpu.make_async_copy(OUT.at[1], outw, s_out.at[1]).start()
 
         return carry
 
-    lax.fori_loop(0, 10, main, 0)
+    lax.fori_loop(0, 11, main, 0)
 
     rt_e.wait_send()
     rt_w.wait_send()
-    drain(WD.at[pl.ds(0, (NJ - 1) * nf)], s_wd.at[0])
+    drain(WD.at[pl.ds(0, (NX - 1) * nf)], s_wd.at[0])
 
     def finish(c, carry):
-        drain(PK.at[c], s_a.at[c])
         for s in level0(c) + level1(c) + level2(c):
             s.wait_send()
-        drain(H.at[c, pl.ds(0, NJ - 1)], s_h.at[c])
-        drain(O.at[c, pl.ds(0, (NJ - 1) * blk)], s_b.at[c])
+        drain(H.at[c, pl.ds(0, NX - 1)], s_h.at[c])
+        to_y(c).wait_send()
+        drain(B.at[c, pl.ds(0, 2 * (NX - 1) * blk)], s_b.at[c])
         drain(C.at[c, pl.ds(0, (nz - 1) * 2 * NJ)], s_f.at[c])
         return carry
 
     lax.fori_loop(0, NCH, finish, 0)
+    drain(PK.at[NCH - 1], s_a.at[NCH - 1])
     pltpu.make_async_copy(OUT.at[0], oute, s_out.at[0]).wait()
     pltpu.make_async_copy(OUT.at[1], outw, s_out.at[1]).wait()
 
@@ -431,15 +465,18 @@
             pltpu.VMEM((2, top, 128), I32),
             pltpu.VMEM((2, top, 128), F32),
             pltpu.VMEM((d, 2 * nf), BF16),
-            pltpu.VMEM((NJ * nf, oc), BF16),
+            pltpu.VMEM((NX * nf, d // NX), BF16),
             pltpu.VMEM((1, d), F32),
             pltpu.VMEM((mr, mr), BF16),
             pltpu.VMEM((mr, mr), BF16),
             pltpu.VMEM((NCH, mr, oc), BF16),
             pltpu.VMEM((NCH, mr, oc), BF16),
             pltpu.VMEM((NCH, NJ, blk, d), BF16),
-            pltpu.VMEM((NCH, NJ, NJ * blk, nf), BF16),
-            pltpu.VMEM((NCH, NJ * blk, oc), BF16),
+            pltpu.VMEM((NCH, NX, NJ * blk, nf), BF16),
+            pltpu.VMEM((NCH, NX * blk, d // NX), BF16),
+            pltpu.VMEM((NCH, NX * blk, d // NX), BF16),
+            pltpu.VMEM((NCH, NX * blk, d // NX), F32),
+            pltpu.VMEM((NCH, NX * blk, d // NX), BF16),
             pltpu.VMEM((NCH, NJ * blk, oc), BF16),
             pltpu.VMEM((NCH, mr, oc), BF16),
             pltpu.VMEM((NCH, mr, oc), BF16),
@@ -461,9 +498,11 @@
             dma((NCH,)),
             dma((NCH,)),
             dma((NCH,)),
+            dma((NCH,)),
+            dma((NCH,)),
         ],
         compiler_params=pltpu.CompilerParams(
-            collective_id=0, has_side_effects=True, vmem_limit_bytes=48 * 2**20
+            collective_id=0, has_side_effects=True, vmem_limit_bytes=63 * 2**20
         ),
         cost_estimate=pl.CostEstimate(flops=flops, bytes_accessed=moved, transcendentals=0),
     )(

time: 138 us -> 120 us (0.87)
  Pallas kernels: 127 us -> 116 us
  local copies, waits for them, and re-layouts: 9.88 us -> 3.17 us
    pallas_call x1, Pallas kernels: 127 us -> 116 us  [body(): pl.pallas_call(functools.partial(kernel, np_, nz, d, tok, nf), out_shape=...]
    unnamed x20 -> x4, local copies, waits for them, and re-layouts: 9.88 us -> 3.17 us
where the time goes in v2:
time: 120 us
  Pallas kernels  116 us (97%)
  local copies, waits for them, and re-layouts  3.17 us (3%)
    pallas_call x1, Pallas kernels, body(): pl.pallas_call(functools.partial(kernel, np_, nz, d, tok, nf), out_shape=...  116 us
    unnamed x4, local copies, waits for them, and re-layouts  3.17 us

profile of v2, /device:TPU:1, one launch (start us, length us, event | category | flops | bytes accessed | tf_op | source)
XLA Modules:
  0.0 119.7 jit_solution(15898138419157067060)
XLA Ops:
  0.6 115.9 %shard_map.122 = (bf16[64,7168]{1,0:T(8,128)(2,1)}, bf16[64,7168]{1,0:T(8,128)(2,1)}) custom-call(bf16[64,7168]{1,0:T(8,128)(2,1)} %bitcast.25, bf16[64,7168]{1,0:T(8,128)(2,1)} %bitcast.26, s32[8,64]{1,0:T(8,128)} %bitcast.27, s32[8,64]{1,0:T(8,128)} %bitcast.28, f32[8,64]{1,0:T(8,128)} %bitcast.29, f32[8,64]{1,0:T(8,128)} %bitcast.30, f32[1,7168]{1,0:T(1,128)} %gain.1, ...), custom_call_target="tpu_custom_call" | custom-call | flops 2818572288 | bytes 18350080 | tf_op jit(solution)/shard_map/pallas_call | solution.py:456
  116.5 0.0 copy-start
  116.5 2.2 %copy.15 = bf16[1,64,7168]{2,1,0:T(8,128)(2,1)} copy(bf16[1,64,7168]{2,1,0:T(8,128)(2,1)} %bitcast.21) | data formatting | bytes 1835008
  118.8 0.0 copy-done
  118.8 0.9 copy.16
Async XLA Ops:
  116.5 2.3 %copy-start = (bf16[64,7168]{1,0:T(8,128)(2,1)S(1)}, bf16[64,7168]{1,0:T(8,128)(2,1)}, u32[]{:S(2)}) copy-start(bf16[64,7168]{1,0:T(8,128)(2,1)} %get-tuple-element.5) | copy-start | bytes 2752516

commit v3 on v2

--- a/solution.py
+++ b/solution.py
@@ -218,7 +218,7 @@
         for o in range(NJ):
             v = u[o * blk : (o + 1) * blk]
             G[c, j, :, o * oc : (o + 1) * oc] = (v * inv * GS[:, o * oc : (o + 1) * oc]).astype(BF16)
-        for s in level0(c):
+        for s in level0(c)[::-1]:
             s.start()
 
     def stage_l1(c):
@@ -354,7 +354,7 @@
 
     def pack_loop(c, carry):
         stage_a(c)
-        pl.when(c == 0)(lambda: send_a(c))
+        send_a(c)
         return carry
 
     lax.fori_loop(0, NCH, pack_loop, 0)
@@ -386,11 +386,6 @@
             c = it - lag
             pl.when((c >= 0) & (c < NCH))(lambda: f(c))
 
-        def next_a(c):
-            drain(PK.at[c], s_a.at[c])
-            send_a(c + 1)
-
-        pl.when(it < NCH - 1)(lambda: next_a(it))
         when(0, stage_b)
         when(1, stage_l1)
         when(2, stage_l2)
@@ -435,7 +430,8 @@
         return carry
 
     lax.fori_loop(0, NCH, finish, 0)
-    drain(PK.at[NCH - 1], s_a.at[NCH - 1])
+    for c in range(NCH):
+        drain(PK.at[c], s_a.at[c])
     pltpu.make_async_copy(OUT.at[0], oute, s_out.at[0]).wait()
     pltpu.make_async_copy(OUT.at[1], outw, s_out.at[1]).wait()
 

time: 120 us -> 119 us (level)
  no operation moved by 1% of the time
where the time goes in v3:
time: 119 us
  Pallas kernels  115 us (97%)
  local copies, waits for them, and re-layouts  3.17 us (3%)
    pallas_call x1, Pallas kernels, body(): pl.pallas_call(functools.partial(kernel, np_, nz, d, tok, nf), out_shape=...  115 us
    unnamed x4, local copies, waits for them, and re-layouts  3.17 us

profile of v3, /device:TPU:1, one launch (start us, length us, event | category | flops | bytes accessed | tf_op | source)
XLA Modules:
  0.0 118.6 jit_solution(16574602626914152247)
XLA Ops:
  0.6 114.7 %shard_map.122 = (bf16[64,7168]{1,0:T(8,128)(2,1)}, bf16[64,7168]{1,0:T(8,128)(2,1)}) custom-call(bf16[64,7168]{1,0:T(8,128)(2,1)} %bitcast.25, bf16[64,7168]{1,0:T(8,128)(2,1)} %bitcast.26, s32[8,64]{1,0:T(8,128)} %bitcast.27, s32[8,64]{1,0:T(8,128)} %bitcast.28, f32[8,64]{1,0:T(8,128)} %bitcast.29, f32[8,64]{1,0:T(8,128)} %bitcast.30, f32[1,7168]{1,0:T(1,128)} %gain.1, ...), custom_call_target="tpu_custom_call" | custom-call | flops 2818572288 | bytes 18350080 | tf_op jit(solution)/shard_map/pallas_call | solution.py:452
  115.4 0.0 copy-start
  115.4 2.2 %copy.15 = bf16[1,64,7168]{2,1,0:T(8,128)(2,1)} copy(bf16[1,64,7168]{2,1,0:T(8,128)(2,1)} %bitcast.21) | data formatting | bytes 1835008
  117.6 0.0 copy-done
  117.6 0.9 copy.16
Async XLA Ops:
  115.4 2.3 %copy-start = (bf16[64,7168]{1,0:T(8,128)(2,1)S(1)}, bf16[64,7168]{1,0:T(8,128)(2,1)}, u32[]{:S(2)}) copy-start(bf16[64,7168]{1,0:T(8,128)(2,1)} %get-tuple-element.5) | copy-start | bytes 2752516

commit v4 on v3

--- a/solution.py
+++ b/solution.py
@@ -21,10 +21,10 @@
 
 def kernel(
     np_, nz, d, tok, nf,
-    xe, xw, rte, rtw, afe, afw, gain, wg, wu, wd, scales,
+    xe, xw, rte, rtw, afe, afw, gain_in, wg, wu, wd, scales,
     oute, outw,
-    X, RP, RR, AP, W, WD, GS, T1, T2, PK, Q, G, H, OY, YR, PF, SR, B, C, F, SP, OUT,
-    s_loc, s_out, s_rt, r_rt, s_wd, r_wd, s_a, r_a, s_g, r_g, s_h, r_h, s_y, r_y, s_b, r_b, s_f, r_f,
+    RS, AS, gain, X, RP, RR, AP, W, WD, GS, T1, T2, PK, Q, G, H, OY, YR, PF, SR, B, C, F, SP, OUT,
+    s_small, s_loc, s_out, s_rt, r_rt, s_wd, r_wd, s_a, r_a, s_g, r_g, s_h, r_h, s_y, r_y, s_b, r_b, s_f, r_f,
 ):
     oc = d // NJ
     qc = d // NX
@@ -66,6 +66,15 @@
             t = (x + k) % NX
             send(t, (p, base + y * NX + t))
 
+    small = [
+        pltpu.make_async_copy(rte, RS.at[0], s_small.at[0]),
+        pltpu.make_async_copy(rtw, RS.at[1], s_small.at[1]),
+        pltpu.make_async_copy(afe, AS.at[0], s_small.at[2]),
+        pltpu.make_async_copy(afw, AS.at[1], s_small.at[3]),
+        pltpu.make_async_copy(gain_in, gain, s_small.at[4]),
+    ]
+    for c in small:
+        c.start()
     local = [
         pltpu.make_async_copy(xe, X.at[0], s_loc.at[0]),
         pltpu.make_async_copy(xw, X.at[1], s_loc.at[1]),
@@ -102,12 +111,14 @@
     on_row(greet)
     greet(x, dev_y)
 
+    for c in small:
+        c.wait()
     RP[...] = jnp.full(RP.shape, -1, I32)
-    RP[0, :, 0:tok] = rte[...]
-    RP[1, :, 0:tok] = rtw[...]
+    RP[0, :, 0:tok] = RS[0]
+    RP[1, :, 0:tok] = RS[1]
     AP[...] = jnp.full(AP.shape, 1.0, F32)
-    AP[0, :, 0:tok] = afe[...]
-    AP[1, :, 0:tok] = afw[...]
+    AP[0, :, 0:tok] = AS[0]
+    AP[1, :, 0:tok] = AS[1]
 
     pl.semaphore_wait(bar, 2 * nz + (nz - 1) + NX)
 
@@ -445,17 +456,19 @@
     mr = nz * NJ * 2
     blk = 2 * nz
     top = rte.shape[2]
-    any_, vm = pl.BlockSpec(memory_space=pl.ANY), pl.BlockSpec(memory_space=pltpu.VMEM)
+    any_, hbm = pl.BlockSpec(memory_space=pl.ANY), pl.BlockSpec(memory_space=pltpu.HBM)
     dma = pltpu.SemaphoreType.DMA
     flops = 2 * NCH * NJ * blk * d * 3 * nf
     moved = 2 * 2 * (4 * tok * d + 3 * d * nf)
     outs = pl.pallas_call(
         functools.partial(kernel, np_, nz, d, tok, nf),
         out_shape=[jax.ShapeDtypeStruct((tok, d), BF16)] * 2,
-        in_specs=[any_, any_, vm, vm, vm, vm, vm, any_, any_, any_]
-        + [pl.BlockSpec(memory_space=pltpu.SMEM)],
+        in_specs=[hbm] * 10 + [pl.BlockSpec(memory_space=pltpu.SMEM)],
         out_specs=[any_, any_],
         scratch_shapes=[
+            pltpu.VMEM((2, top, tok), I32),
+            pltpu.VMEM((2, top, tok), F32),
+            pltpu.VMEM((1, d), F32),
             pltpu.VMEM((2, tok, d), BF16),
             pltpu.VMEM((2, top, 128), I32),
             pltpu.VMEM((2, top, 128), I32),
@@ -479,6 +492,7 @@
             pltpu.VMEM((2, 2, NJ * tok, 2 * mr), BF16),
             pltpu.VMEM((2, tok, d), BF16),
             dma((5,)),
+            dma((5,)),
             dma((2,)),
             dma((2,)),
             dma((2,)),
@@ -498,7 +512,7 @@
             dma((NCH,)),
         ],
         compiler_params=pltpu.CompilerParams(
-            collective_id=0, has_side_effects=True, vmem_limit_bytes=63 * 2**20
+            collective_id=0, has_side_effects=True, vmem_limit_bytes=56 * 2**20
         ),
         cost_estimate=pl.CostEstimate(flops=flops, bytes_accessed=moved, transcendentals=0),
     )(

time: 119 us -> 119 us (level)
  no operation moved by 1% of the time
where the time goes in v4:
time: 119 us
  Pallas kernels  115 us (97%)
  local copies, waits for them, and re-layouts  3.17 us (3%)
    pallas_call x1, Pallas kernels, body(): pl.pallas_call(functools.partial(kernel, np_, nz, d, tok, nf), out_shape=...  115 us
    unnamed x4, local copies, waits for them, and re-layouts  3.17 us

profile of v4, /device:TPU:1, one launch (start us, length us, event | category | flops | bytes accessed | tf_op | source)
XLA Modules:
  0.0 118.6 jit_solution(9352578424251472214)
XLA Ops:
  0.6 114.8 %shard_map.122 = (bf16[64,7168]{1,0:T(8,128)(2,1)}, bf16[64,7168]{1,0:T(8,128)(2,1)}) custom-call(bf16[64,7168]{1,0:T(8,128)(2,1)} %bitcast.25, bf16[64,7168]{1,0:T(8,128)(2,1)} %bitcast.26, s32[8,64]{1,0:T(8,128)} %bitcast.27, s32[8,64]{1,0:T(8,128)} %bitcast.28, f32[8,64]{1,0:T(8,128)} %bitcast.29, f32[8,64]{1,0:T(8,128)} %bitcast.30, f32[1,7168]{1,0:T(1,128)} %gain_in.1, ...), custom_call_target="tpu_custom_call" | custom-call | flops 2818572288 | bytes 18350080 | tf_op jit(solution)/shard_map/pallas_call | solution.py:463
  115.4 0.0 copy-start
  115.4 2.2 %copy.15 = bf16[1,64,7168]{2,1,0:T(8,128)(2,1)} copy(bf16[1,64,7168]{2,1,0:T(8,128)(2,1)} %bitcast.21) | data formatting | bytes 1835008
  117.7 0.0 copy-done
  117.7 0.9 copy.16
Async XLA Ops:
  115.4 2.3 %copy-start = (bf16[64,7168]{1,0:T(8,128)(2,1)S(1)}, bf16[64,7168]{1,0:T(8,128)(2,1)}, u32[]{:S(2)}) copy-start(bf16[64,7168]{1,0:T(8,128)(2,1)} %get-tuple-element.5) | copy-start | bytes 2752516
